TPU v7x, 32 devices: a whole 2x2x4 slice. The times are simulated.
32 devices in a mesh: grp: 2 (over x), band: 16 (over z, y, core).
Axes of the slice: x: 2, y: 2, z: 4, core: 2. Of those that a mesh axis runs over, the one named last changes fastest.
Arguments:
- orbitals: float32 [6, 64, 128, 128], P('grp', 'band'), parts along dimension 0, may hold values from -6 to 6
- band_ids: int32 [6], P('grp'), parts along dimension 0, may hold values from 0 to 2, each once
- occupations: float32 [6], P('grp'), parts along dimension 0, may hold values from 0.1 to 1
- screen: float32 [64, 128, 128], P('band'), may hold values from 0.2 to 2
Outputs:
- exchange: float32 [6, 64, 128, 128], P('grp', 'band'), parts along dimension 0
- energy: float32 [2], P('grp'), parts along dimension 0
There are 2 independent parts, one for each index of `grp`. A program takes and returns all parts, laid end to end along the dimension named above; an argument that names none is the same for every part. Nothing has to cross between parts.
Inputs may be any that keep to these rules, and one draw needn't show every extreme that they name: `band_ids`: each band number appears in exactly one slot.
All inputs are finite; a program needn't handle non-finite values.
Results may differ from a plain program's by a relative error of at most 0.00002.
Values sent between devices are 32-bit elements; how exact they have to be, the bound alone decides.
A program may use at most 64 MiB of HBM per device.

v0:
```python
import jax
import jax.numpy as jnp
from jax import lax
from jax.sharding import PartitionSpec as P

SWEEPS = 4


def padded_2(block, sides, width):
    for axis, dim in sides:
        count = lax.axis_size(axis)
        forward = [(i, i + 1) for i in range(count - 1)]
        backward = [(target, source) for source, target in forward]
        low = lax.ppermute(
            lax.slice_in_dim(block, block.shape[dim] - width, None, axis=dim), axis, forward
        )
        high = lax.ppermute(lax.slice_in_dim(block, 0, width, axis=dim), axis, backward)
        block = jnp.concatenate([low, block, high], axis=dim)
    return block


def relax(phi, padded_x, rho, diag):
    lead = ((0, 0),) * (phi.ndim - 3)
    padded = jnp.pad(padded_x, lead + ((0, 0), (1, 1), (1, 1)))
    near = padded[..., 2:, 1:-1, 1:-1] + padded[..., :-2, 1:-1, 1:-1]
    near = near + padded[..., 1:-1, 2:, 1:-1] + padded[..., 1:-1, :-2, 1:-1]
    near = near + padded[..., 1:-1, 1:-1, 2:] + padded[..., 1:-1, 1:-1, :-2]
    return phi + 0.8 * (rho - (diag * phi - near)) / diag


def pad_planes(phi):
    lead = ((0, 0),) * (phi.ndim - 3)
    return jnp.pad(phi, lead + ((1, 1), (0, 0), (0, 0)))


def body(orbitals, band_ids, occupations, screen):
    planes = orbitals.shape[1]
    total = occupations.shape[0]
    lookup = (band_ids[:, None] == jnp.arange(total, dtype=jnp.int32)[None, :]).astype(jnp.float32)
    occ = jnp.sum(lookup * occupations[None, :], axis=1)
    weighted = occ[:, None, None, None] * orbitals
    diag = 6.0 + screen
    rho = orbitals[:, None] * orbitals[None]
    phi = jnp.zeros_like(rho)
    for sweep in range(SWEEPS):
        if sweep == 0:
            padded_x = pad_planes(phi)
        else:
            padded_x = padded_2(phi, (("band", 2),), 1)
        phi = relax(phi, padded_x, rho, diag)
    exchange = -jnp.sum(weighted[None] * phi, axis=1)
    cells = planes * lax.axis_size("band") * orbitals.shape[2] * orbitals.shape[3]
    local = 0.5 / cells * jnp.sum(weighted * exchange)
    energy = lax.psum(local, "band")
    return (exchange, energy.reshape(1))


def solution(mesh):
    in_specs = (P("grp", "band", None, None), P("grp"), P("grp"), P("band", None, None))
    out_specs = (P("grp", "band", None, None), P("grp"))
    return jax.shard_map(body, mesh=mesh, in_specs=in_specs, out_specs=out_specs, check_vma=False)
```

profile of v0, /device:TPU:0, one launch (start us, length us, event | category | flops | bytes accessed | tf_op | source)
XLA Modules:
  0.0 108.3 jit_solution(14066808430868312300)
XLA Ops:
  0.8 1.1 broadcast_multiply_fusion.1
  1.9 0.4 pad.23
  2.3 1.4 %fusion.4 = f32[3,3,4,128,128]{4,3,2,1,0:T(8,128)S(1)} fusion(f32[3,3,6,128,128]{4,3,2,1,0:T(8,128)S(1)} %pad.23, f32[4,128,128]{2,1,0:T(8,128)S(1)} %get-tuple-element.11, f32[4]{0:T(128)S(1)} %slice_add_fusion.12, f32[4,128,128]{2,1,0:T(8,128)S(1)} %get-tuple-element.10, f32[3,4,128,128]{3,2,1,0:T(8,128)S(1)} %copy-done), kind=kLoop, calls=%fused_computation.22 | loop fusion | flops 5308416 | bytes 7995904 | tf_op jit(solution)/shard_map/div | solution.py:28
  3.7 0.1 fusion.29
  3.8 1.3 %collective-permute-start = (f32[3,3,1,128,128]{4,3,2,1,0:T(8,128)S(1)}, f32[3,3,1,128,128]{4,3,2,1,0:T(8,128)S(1)}, u32[]{:S(2)}, u32[]{:S(2)}) collective-permute-start(f32[3,3,1,128,128]{4,3,2,1,0:T(8,128)S(1)} %get-tuple-element.9), channel_id=1, source_target_pairs={{1,0},{2,1},{3,2},{4,3},{5,4},{6,5},{7,6},{8,7},{9,8},{10,9},{11,1... | collective-permute-start | bytes 1769480 | tf_op jit(solution)/shard_map/ppermute | solution.py:17
  5.1 3.1 %collective-permute-start.1 = (f32[3,3,1,128,128]{4,3,2,1,0:T(8,128)S(1)}, f32[3,3,1,128,128]{4,3,2,1,0:T(8,128)S(1)}, u32[]{:S(2)}, u32[]{:S(2)}) collective-permute-start(f32[3,3,1,128,128]{4,3,2,1,0:T(8,128)S(1)} %get-tuple-element.8), channel_id=1, source_target_pairs={{0,1},{1,2},{2,3},{3,4},{4,5},{5,6},{6,7},{7,8},{8,9},{9,10},{10,1... | collective-permute-start | bytes 1769480 | tf_op jit(solution)/shard_map/ppermute | solution.py:14
  8.1 1.6 %collective-permute-done.1 = f32[3,3,1,128,128]{4,3,2,1,0:T(8,128)S(1)} collective-permute-done((f32[3,3,1,128,128]{4,3,2,1,0:T(8,128)S(1)}, f32[3,3,1,128,128]{4,3,2,1,0:T(8,128)S(1)}, u32[]{:S(2)}, u32[]{:S(2)}) %collective-permute-start.1) | collective-permute-done | bytes 589856 | tf_op jit(solution)/shard_map/ppermute | solution.py:14
  9.7 3.1 %select_maximum_fusion.4 = f32[3,3,6,130,130]{4,3,2,1,0:T(8,128)S(1)} fusion(f32[3,3,1,128,128]{4,3,2,1,0:T(8,128)S(1)} %collective-permute-done, f32[3,3,4,128,128]{4,3,2,1,0:T(8,128)S(1)} %fusion.4, f32[3,3,1,128,128]{4,3,2,1,0:T(8,128)S(1)} %collective-permute-done.1), kind=kLoop, calls=%fused_computation.12 | loop fusion | flops 13689000 | bytes 7189344 | tf_op jit(solution)/shard_map/concatenate | solution.py:18
  12.9 2.9 %fusion.7 = f32[3,3,4,128,128]{4,3,2,1,0:T(8,128)S(1)} fusion(f32[3,3,4,128,128]{4,3,2,1,0:T(8,128)S(1)} %fusion.4, f32[3,3,6,130,130]{4,3,2,1,0:T(8,128)S(1)} %select_maximum_fusion.4, f32[3,3,1,128,128]{4,3,2,1,0:T(8,128)S(1)} %collective-permute-done.1, f32[3,3,1,128,128]{4,3,2,1,0:T(8,128)S(1)} %collective-permute-done, ...), kind=kLoop, calls=%fused_computation.25 | loop fusion | flops 8257536 | bytes 17170432 | tf_op jit(solution)/shard_map/add | solution.py:28
  15.8 1.3 %collective-permute-start.2 = (f32[3,3,1,128,128]{4,3,2,1,0:T(8,128)S(1)}, f32[3,3,1,128,128]{4,3,2,1,0:T(8,128)S(1)}, u32[]{:S(2)}, u32[]{:S(2)}) collective-permute-start(f32[3,3,1,128,128]{4,3,2,1,0:T(8,128)S(1)} %get-tuple-element.7), channel_id=1, source_target_pairs={{1,0},{2,1},{3,2},{4,3},{5,4},{6,5},{7,6},{8,7},{9,8},{10,9},{11,1... | collective-permute-start | bytes 1769480 | tf_op jit(solution)/shard_map/ppermute | solution.py:17
  17.1 15.7 %collective-permute-start.3 = (f32[3,3,1,128,128]{4,3,2,1,0:T(8,128)S(1)}, f32[3,3,1,128,128]{4,3,2,1,0:T(8,128)S(1)}, u32[]{:S(2)}, u32[]{:S(2)}) collective-permute-start(f32[3,3,1,128,128]{4,3,2,1,0:T(8,128)S(1)} %get-tuple-element.6), channel_id=1, source_target_pairs={{0,1},{1,2},{2,3},{3,4},{4,5},{5,6},{6,7},{7,8},{8,9},{9,10},{10,1... | collective-permute-start | bytes 1769480 | tf_op jit(solution)/shard_map/ppermute | solution.py:14
  32.8 1.6 %collective-permute-done.3 = f32[3,3,1,128,128]{4,3,2,1,0:T(8,128)S(1)} collective-permute-done((f32[3,3,1,128,128]{4,3,2,1,0:T(8,128)S(1)}, f32[3,3,1,128,128]{4,3,2,1,0:T(8,128)S(1)}, u32[]{:S(2)}, u32[]{:S(2)}) %collective-permute-start.3) | collective-permute-done | bytes 589856 | tf_op jit(solution)/shard_map/ppermute | solution.py:14
  34.4 3.1 %select_maximum_fusion.2 = f32[3,3,6,130,130]{4,3,2,1,0:T(8,128)S(1)} fusion(f32[3,3,1,128,128]{4,3,2,1,0:T(8,128)S(1)} %collective-permute-done.2, f32[3,3,4,128,128]{4,3,2,1,0:T(8,128)S(1)} %fusion.7, f32[3,3,1,128,128]{4,3,2,1,0:T(8,128)S(1)} %collective-permute-done.3), kind=kLoop, calls=%fused_computation.10 | loop fusion | flops 13689000 | bytes 7189344 | tf_op jit(solution)/shard_map/concatenate | solution.py:18
  37.5 2.9 %fusion.10 = f32[3,3,4,128,128]{4,3,2,1,0:T(8,128)S(1)} fusion(f32[3,3,4,128,128]{4,3,2,1,0:T(8,128)S(1)} %fusion.7, f32[3,3,6,130,130]{4,3,2,1,0:T(8,128)S(1)} %select_maximum_fusion.2, f32[3,3,1,128,128]{4,3,2,1,0:T(8,128)S(1)} %collective-permute-done.3, f32[3,3,1,128,128]{4,3,2,1,0:T(8,128)S(1)} %collective-permute-done.2, ...), kind=kLoop, calls=%fused_computation.28 | loop fusion | flops 8257536 | bytes 17170432 | tf_op jit(solution)/shard_map/add | solution.py:28
  40.4 0.1 fusion.27
  40.5 1.3 %collective-permute-start.4 = (f32[3,3,1,128,128]{4,3,2,1,0:T(8,128)S(1)}, f32[3,3,1,128,128]{4,3,2,1,0:T(8,128)S(1)}, u32[]{:S(2)}, u32[]{:S(2)}) collective-permute-start(f32[3,3,1,128,128]{4,3,2,1,0:T(8,128)S(1)} %get-tuple-element.5), channel_id=1, source_target_pairs={{1,0},{2,1},{3,2},{4,3},{5,4},{6,5},{7,6},{8,7},{9,8},{10,9},{11,1... | collective-permute-start | bytes 1769480 | tf_op jit(solution)/shard_map/ppermute | solution.py:17
  41.8 11.3 %collective-permute-start.5 = (f32[3,3,1,128,128]{4,3,2,1,0:T(8,128)S(1)}, f32[3,3,1,128,128]{4,3,2,1,0:T(8,128)S(1)}, u32[]{:S(2)}, u32[]{:S(2)}) collective-permute-start(f32[3,3,1,128,128]{4,3,2,1,0:T(8,128)S(1)} %get-tuple-element.4), channel_id=1, source_target_pairs={{0,1},{1,2},{2,3},{3,4},{4,5},{5,6},{6,7},{7,8},{8,9},{9,10},{10,1... | collective-permute-start | bytes 1769480 | tf_op jit(solution)/shard_map/ppermute | solution.py:14
  53.1 0.2 select_reduce_fusion
  53.3 0.2 broadcast_multiply_fusion
  53.4 1.2 %collective-permute-done.5 = f32[3,3,1,128,128]{4,3,2,1,0:T(8,128)S(1)} collective-permute-done((f32[3,3,1,128,128]{4,3,2,1,0:T(8,128)S(1)}, f32[3,3,1,128,128]{4,3,2,1,0:T(8,128)S(1)}, u32[]{:S(2)}, u32[]{:S(2)}) %collective-permute-start.5) | collective-permute-done | bytes 589856 | tf_op jit(solution)/shard_map/ppermute | solution.py:14
  54.6 3.1 %select_maximum_fusion = f32[3,3,6,130,130]{4,3,2,1,0:T(8,128)S(1)} fusion(f32[3,3,1,128,128]{4,3,2,1,0:T(8,128)S(1)} %collective-permute-done.4, f32[3,3,4,128,128]{4,3,2,1,0:T(8,128)S(1)} %fusion.10, f32[3,3,1,128,128]{4,3,2,1,0:T(8,128)S(1)} %collective-permute-done.5), kind=kLoop, calls=%fused_computation.8 | loop fusion | flops 13689000 | bytes 7189344 | tf_op jit(solution)/shard_map/concatenate | solution.py:18
  57.8 2.7 %fusion.26 = f32[3,4,128,128]{3,2,1,0:T(8,128)S(1)} fusion(f32[3,3,4,128,128]{4,3,2,1,0:T(8,128)S(1)} %fusion.10, f32[3,3,6,130,130]{4,3,2,1,0:T(8,128)S(1)} %select_maximum_fusion, f32[3,3,1,128,128]{4,3,2,1,0:T(8,128)S(1)} %collective-permute-done.5, f32[3,3,1,128,128]{4,3,2,1,0:T(8,128)S(1)} %collective-permute-done.4, ...), kind=kLoop, calls=%fused_computation.62 | loop fusion | flops 9240576 | bytes 16384000 | tf_op jit(solution)/shard_map/reduce_sum | solution.py:51
  60.5 1.5 %multiply_reduce_fusion = (f32[]{:T(128)}, f32[3,4,128,128]{3,2,1,0:T(8,128)}) fusion(f32[3,4,128,128]{3,2,1,0:T(8,128)S(1)} %fusion.26, f32[3,4,128,128]{3,2,1,0:T(8,128)S(1)} %copy-done, f32[3]{0:T(128)S(1)} %select_reduce_fusion), kind=kLoop, calls=%fused_computation.63 | loop fusion | flops 786431 | bytes 2359312 | tf_op jit(solution)/shard_map/reduce_sum | solution.py:53
  62.7 45.6 %psum.7 = f32[1]{0:T(128)} all-reduce(f32[1]{0:T(128)} %bitcast), channel_id=1, replica_groups=mesh['grp'=2,'band'=16] {'band'}, use_global_device_ids=true, to_apply=%region_3.4 | all-reduce | flops 1 | bytes 8 | tf_op jit(solution)/shard_map/psum | solution.py:54
  (13 shorter events, 0.3 us)
Async XLA Ops:
  0.6 1.7 %copy-start = (f32[3,4,128,128]{3,2,1,0:T(8,128)S(1)}, f32[3,4,128,128]{3,2,1,0:T(8,128)}, u32[]{:S(2)}) copy-start(f32[3,4,128,128]{3,2,1,0:T(8,128)} %param.4) | copy-start | bytes 2359300
  3.8 4.4 %collective-permute-start = (f32[3,3,1,128,128]{4,3,2,1,0:T(8,128)S(1)}, f32[3,3,1,128,128]{4,3,2,1,0:T(8,128)S(1)}, u32[]{:S(2)}, u32[]{:S(2)}) collective-permute-start(f32[3,3,1,128,128]{4,3,2,1,0:T(8,128)S(1)} %get-tuple-element.9), channel_id=1, source_target_pairs={{1,0},{2,1},{3,2},{4,3},{5,4},{6,5},{7,6},{8,7},{9,8},{10,9},{11,1... | collective-permute-start | bytes 1769480 | tf_op jit(solution)/shard_map/ppermute | solution.py:17
  5.1 4.7 %collective-permute-start.1 = (f32[3,3,1,128,128]{4,3,2,1,0:T(8,128)S(1)}, f32[3,3,1,128,128]{4,3,2,1,0:T(8,128)S(1)}, u32[]{:S(2)}, u32[]{:S(2)}) collective-permute-start(f32[3,3,1,128,128]{4,3,2,1,0:T(8,128)S(1)} %get-tuple-element.8), channel_id=1, source_target_pairs={{0,1},{1,2},{2,3},{3,4},{4,5},{5,6},{6,7},{7,8},{8,9},{9,10},{10,1... | collective-permute-start | bytes 1769480 | tf_op jit(solution)/shard_map/ppermute | solution.py:14
  15.8 17.0 %collective-permute-start.2 = (f32[3,3,1,128,128]{4,3,2,1,0:T(8,128)S(1)}, f32[3,3,1,128,128]{4,3,2,1,0:T(8,128)S(1)}, u32[]{:S(2)}, u32[]{:S(2)}) collective-permute-start(f32[3,3,1,128,128]{4,3,2,1,0:T(8,128)S(1)} %get-tuple-element.7), channel_id=1, source_target_pairs={{1,0},{2,1},{3,2},{4,3},{5,4},{6,5},{7,6},{8,7},{9,8},{10,9},{11,1... | collective-permute-start | bytes 1769480 | tf_op jit(solution)/shard_map/ppermute | solution.py:17
  17.1 17.2 %collective-permute-start.3 = (f32[3,3,1,128,128]{4,3,2,1,0:T(8,128)S(1)}, f32[3,3,1,128,128]{4,3,2,1,0:T(8,128)S(1)}, u32[]{:S(2)}, u32[]{:S(2)}) collective-permute-start(f32[3,3,1,128,128]{4,3,2,1,0:T(8,128)S(1)} %get-tuple-element.6), channel_id=1, source_target_pairs={{0,1},{1,2},{2,3},{3,4},{4,5},{5,6},{6,7},{7,8},{8,9},{9,10},{10,1... | collective-permute-start | bytes 1769480 | tf_op jit(solution)/shard_map/ppermute | solution.py:14
  40.4 12.7 %copy-start.1 = (f32[3]{0:T(128)S(1)}, f32[3]{0:T(128)}, u32[]{:S(2)}) copy-start(f32[3]{0:T(128)} %param.6) | copy-start | bytes 40
  40.4 12.7 %copy-start.2 = (s32[3]{0:T(128)S(1)}, s32[3]{0:T(128)}, u32[]{:S(2)}) copy-start(s32[3]{0:T(128)} %param.5) | copy-start | bytes 40
  40.5 12.9 %collective-permute-start.4 = (f32[3,3,1,128,128]{4,3,2,1,0:T(8,128)S(1)}, f32[3,3,1,128,128]{4,3,2,1,0:T(8,128)S(1)}, u32[]{:S(2)}, u32[]{:S(2)}) collective-permute-start(f32[3,3,1,128,128]{4,3,2,1,0:T(8,128)S(1)} %get-tuple-element.5), channel_id=1, source_target_pairs={{1,0},{2,1},{3,2},{4,3},{5,4},{6,5},{7,6},{8,7},{9,8},{10,9},{11,1... | collective-permute-start | bytes 1769480 | tf_op jit(solution)/shard_map/ppermute | solution.py:17
  41.8 12.8 %collective-permute-start.5 = (f32[3,3,1,128,128]{4,3,2,1,0:T(8,128)S(1)}, f32[3,3,1,128,128]{4,3,2,1,0:T(8,128)S(1)}, u32[]{:S(2)}, u32[]{:S(2)}) collective-permute-start(f32[3,3,1,128,128]{4,3,2,1,0:T(8,128)S(1)} %get-tuple-element.4), channel_id=1, source_target_pairs={{0,1},{1,2},{2,3},{3,4},{4,5},{5,6},{6,7},{7,8},{8,9},{9,10},{10,1... | collective-permute-start | bytes 1769480 | tf_op jit(solution)/shard_map/ppermute | solution.py:14
where the time goes:
time: 109 us; the launch traced here: 108 us
  blocking collectives  45.6 us (42%)
  starting transfers between devices  33.9 us (31%)
  other arithmetic  22.2 us (20%)
  waiting for transfers between devices  4.34 us (4%)
  between operations  1.51 us (1%)
    psum x1, blocking collectives, body(): energy = lax.psum(local, 'band')  45.6 us
    ppermute x3, starting transfers between devices, padded_2(): lax.ppermute(lax.slice_in_dim(block, block.shape[dim] - width, None, axis...  30 us
    concatenate x3, other arithmetic, padded_2(): block = jnp.concatenate([low, block, high], axis=dim)  9.42 us
    add x2, other arithmetic, relax(): return phi + 0.8 * (rho - (diag * phi - near)) / diag  5.71 us
    ppermute x3, waiting for transfers between devices, padded_2(): lax.ppermute(lax.slice_in_dim(block, block.shape[dim] - width, None, axis...  4.33 us
    ppermute x3, starting transfers between devices, padded_2(): lax.ppermute(lax.slice_in_dim(block, 0, width, axis=dim), axis, backward)  3.88 us
    reduce_sum x1, other arithmetic, body(): exchange = -jnp.sum(weighted[None] * phi, axis=1)  2.74 us
  transfers between devices with their start and end apart: 6, of which 3 were waited for; matrix products, arithmetic and copies ran while one was open for 0% of the time, Pallas kernels for 0%

commit v1 on v0

v1 whole, which is shorter than its diff:
```python
import functools

import jax
import jax.numpy as jnp
from jax import lax
from jax.experimental import pallas as pl
from jax.experimental.pallas import tpu as pltpu
from jax.sharding import PartitionSpec as P

LO, HI = 0, 1
PAD = 8


def radices_of(count):
    out = []
    while count > 1:
        radix = 4 if count % 4 == 0 else (2 if count % 2 == 0 else count)
        out.append(radix)
        count //= radix
    return out


def kernel(
    dims, cells,
    psi_hbm, screen_hbm, ids_ref, occs_ref, exch_hbm, energy_ref,
    psi, scr, c, usend, urecv, f1, f2, f3, ex, eslots,
    local_sem, out_sem, send_sem, recv_sem, fsend_sem, frecv_sem, esend_sem, erecv_sem,
):
    ngrp, n, nb, planes, gy, gz = dims
    pairs = [(i, j) for i in range(nb) for j in range(i, nb)]
    me = lax.axis_index("band")
    grp = lax.axis_index("grp")
    has = (me > 0, me < n - 1)
    near = (me - 1, me + 1)
    radices = radices_of(n)

    load_psi = pltpu.make_async_copy(psi_hbm, psi.at[:, pl.ds(2, planes)], local_sem.at[0])
    load_scr = pltpu.make_async_copy(screen_hbm, scr, local_sem.at[1])
    load_scr.start()
    load_psi.start()

    def rounds():
        stride, base = 1, 0
        for number, radix in enumerate(radices):
            digit = (me // stride) % radix
            peers = []
            for k in range(1, radix):
                other = (digit + k) % radix
                peers.append((k, other, me + (other - digit) * stride))
            yield number, base, radix, digit, peers
            base += radix
            stride *= radix

    barrier = pltpu.get_barrier_semaphore()
    for side in (LO, HI):
        @pl.when(has[side])
        def _():
            pl.semaphore_signal(barrier, inc=1, device_id={"band": near[side]})
    others = 0
    if ngrp == 2:
        pl.semaphore_signal(barrier, inc=1, device_id={"grp": 1 - grp})
        others += 1
    for _, _, _, _, peers in rounds():
        for _, _, peer in peers:
            pl.semaphore_signal(barrier, inc=1, device_id={"band": peer})
            others += 1
    pl.semaphore_wait(barrier, others + has[LO].astype(jnp.int32) + has[HI].astype(jnp.int32))

    rows = gy // 2 if ngrp == 2 else gy
    mine = pl.ds(pl.multiple_of(grp * rows, 8), rows) if ngrp == 2 else pl.ds(0, gy)
    theirs = pl.ds(pl.multiple_of((1 - grp) * rows, 8), rows) if ngrp == 2 else pl.ds(0, gy)

    def halo(side, depth):
        return 2 - depth if side == LO else planes + 1 + depth

    def own(side, depth):
        return planes - depth if side == LO else depth - 1

    def copy(side, number):
        depth = number // 2 + 1
        if number == 4:
            src, dst = usend.at[side], urecv.at[side]
        elif number % 2 == 0:
            src = psi_hbm.at[:, pl.ds(own(side, depth), 1)]
            dst = psi.at[:, pl.ds(halo(side, depth), 1)]
        else:
            src = c.at[own(side, depth) + 2, mine]
            dst = c.at[halo(side, depth), mine]
        return pltpu.make_async_remote_copy(
            src_ref=src, dst_ref=dst,
            send_sem=send_sem.at[side, number], recv_sem=recv_sem.at[side, number],
            device_id={"band": near[1 - side]},
        )

    def send(number):
        for side in (LO, HI):
            @pl.when(has[1 - side])
            def _():
                copy(side, number).start()

    def arrived(number):
        for side in (LO, HI):
            @pl.when(has[side])
            def _():
                copy(side, number).wait_recv()

    def forward(side, depth, rows_at):
        where = c.at[halo(side, depth), rows_at]
        return pltpu.make_async_remote_copy(
            src_ref=where, dst_ref=where,
            send_sem=fsend_sem.at[side, depth - 1], recv_sem=frecv_sem.at[side, depth - 1],
            device_id={"grp": 1 - grp},
        )

    def screen_arrived(depth):
        arrived(2 * depth - 1)
        if ngrp == 2:
            for side in (LO, HI):
                @pl.when(has[side])
                def _():
                    forward(side, depth, mine).start()
            for side in (LO, HI):
                @pl.when(has[side])
                def _():
                    forward(side, depth, theirs).wait_recv()

    send(0)
    load_scr.wait()
    for p in (0, planes - 1):
        c[p + 2] = 0.8 / (6.0 + scr[p])
    send(1)
    send(2)
    for p in range(1, planes - 1):
        c[p + 2] = 0.8 / (6.0 + scr[p])
    send(3)
    load_psi.wait()
    for side in (LO, HI):
        p = own(side, 3) + 2
        root = jnp.sqrt(c[p])
        for b in range(nb):
            usend[side, b] = root * psi[b, p]
    send(4)

    for side in (LO, HI):
        @pl.when(jnp.logical_not(has[side]))
        def _():
            at = 0 if side == LO else planes + 2
            for d in range(2):
                c[at + d] = jnp.zeros((gy, gz), jnp.float32)
                for b in range(nb):
                    psi[b, at + d] = jnp.zeros((gy, gz), jnp.float32)
            for b in range(nb):
                urecv[side, b] = jnp.zeros((gy, gz), jnp.float32)

    occ = []
    for s in range(nb):
        total = jnp.float32(0.0)
        for b in range(nb):
            total = total + jnp.where(ids_ref[s] == b, occs_ref[b], jnp.float32(0.0))
        occ.append(total)

    zeros = jnp.zeros((PAD, gz), jnp.float32)
    for buf in (f1, f2, f3):
        count = buf.shape[1]

        def clear(at, carry, buf=buf, count=count):
            for k in range(len(pairs)):
                buf[k, at, pl.ds(0, PAD)] = zeros
                buf[k, at, pl.ds(PAD + gy, PAD)] = zeros
            return carry

        lax.fori_loop(0, count, clear, 0)

    lanes = lax.broadcasted_iota(jnp.int32, (gy, gz), 1)
    first, last = lanes == 0, lanes == gz - 1

    def pair_of(k):
        i = jnp.int32(0)
        start = jnp.int32(0)
        at = 0
        for b in range(1, nb):
            at += nb - b + 1
            over = (k >= at).astype(jnp.int32)
            i = i + over
            start = start + over * (nb - b + 1)
        return i, i + k - start

    def lateral(buf, k, at):
        mid = buf[k, at, pl.ds(PAD, gy)]
        total = buf[k, at, pl.ds(PAD - 1, gy)] + buf[k, at, pl.ds(PAD + 1, gy)]
        total = total + jnp.where(first, 0.0, pltpu.roll(mid, 1, 1))
        total = total + jnp.where(last, 0.0, pltpu.roll(mid, gz - 1, 1))
        return mid, total

    def plane_pair(lo, hi):
        def each(body):
            def outer(t, carry):
                body(lo + t * (hi - lo), t)
                return carry

            lax.fori_loop(0, 2, outer, 0)

        return each

    def pairwise(body):
        def step(k, carry):
            i, j = pair_of(k)
            body(k, i, j)
            return carry

        lax.fori_loop(0, len(pairs), step, 0)

    def start_sweep(lo, hi):
        def plane(p, t):
            def one(k, i, j):
                f1[k, p, pl.ds(PAD, gy)] = c[p] * (psi[i, p] * psi[j, p])

            pairwise(one)

        plane_pair(lo, hi)(plane)

    def second(lo, hi, outer=False):
        def plane(p, t):
            def one(k, i, j):
                mid, total = lateral(f1, k, p)
                if outer:
                    total = total + f1[k, p + 1 - 2 * t, pl.ds(PAD, gy)]
                else:
                    total = total + f1[k, p - 1, pl.ds(PAD, gy)] + f1[k, p + 1, pl.ds(PAD, gy)]
                f2[k, p, pl.ds(PAD, gy)] = 1.2 * mid + c[p] * total

            pairwise(one)

        plane_pair(lo, hi)(plane)

    def third(lo, hi):
        def plane(p, t):
            def one(k, i, j):
                mid, total = lateral(f2, k, p)
                total = total + f2[k, p - 1, pl.ds(PAD, gy)] + f2[k, p + 1, pl.ds(PAD, gy)]
                total = total + psi[i, p] * psi[j, p]
                f3[k, p - 1, pl.ds(PAD, gy)] = 0.2 * mid + c[p] * total

            pairwise(one)

        plane_pair(lo, hi)(plane)

    def fourth(lo, hi):
        def plane(p, t):
            done = set()
            for k, (i, j) in enumerate(pairs):
                mid, total = lateral(f3, k, p - 1)
                total = total + f3[k, p - 2, pl.ds(PAD, gy)] + f3[k, p, pl.ds(PAD, gy)]
                total = total + psi[i, p] * psi[j, p]
                phi = 0.2 * mid + c[p] * total
                for a, b in {(i, j), (j, i)}:
                    term = (occ[b] * psi[b, p]) * phi
                    ex[a, p - 2] = ex[a, p - 2] - term if a in done else -term
                    done.add(a)

        plane_pair(lo, hi)(plane)

    m = planes - 1 + 2
    start_sweep(2, m)
    start_sweep(3, m - 1)
    second(3, m - 1)
    arrived(0)
    screen_arrived(1)
    start_sweep(1, m + 1)
    second(2, m)
    third(3, m - 1)
    arrived(2)
    screen_arrived(2)
    start_sweep(0, m + 2)
    second(1, m + 1)
    third(2, m)

    def energy_plane(p, acc):
        def one(k, acc):
            i, j = pair_of(k)
            a, b, d = (buf[k, at, pl.ds(PAD, gy)] for buf, at in ((f1, p), (f2, p), (f3, p - 1)))
            weight = jnp.float32(0.0)
            for number, (x, y) in enumerate(pairs):
                weight = jnp.where(k == number, (1.0 if x == y else 2.0) * occ[x] * occ[y], weight)
            value = psi[i, p] * psi[j, p] * b + (b - a) * (d - a) * (1.25 * (6.0 + scr[p - 2]))
            return acc + weight * jnp.sum(value.reshape(gy // 8, 8, gz), axis=0)

        return lax.fori_loop(0, len(pairs), one, acc)

    local = lax.fori_loop(2, planes + 2, energy_plane, jnp.zeros((8, gz), jnp.float32))

    def ecopy(number, base, digit, k, slot, peer):
        return pltpu.make_async_remote_copy(
            src_ref=eslots.at[base + digit], dst_ref=eslots.at[base + slot],
            send_sem=esend_sem.at[base + k], recv_sem=erecv_sem.at[base + slot],
            device_id={"band": peer},
        )

    def esend(entry, value):
        number, base, radix, digit, peers = entry
        eslots[base + digit] = value
        for k, other, peer in peers:
            ecopy(number, base, digit, k, digit, peer).start()

    def ewait(entry):
        number, base, radix, digit, peers = entry
        for k, other, peer in peers:
            ecopy(number, base, digit, k, other, peer).wait_recv()
        total = eslots[base]
        for r in range(1, radix):
            total = total + eslots[base + r]
        return total

    schedule = list(rounds())
    if schedule:
        esend(schedule[0], local)

    second(0, m + 2, outer=True)
    third(1, m + 1)
    fourth(3, m - 1)

    def out_copy(p, slot):
        return pltpu.make_async_copy(
            ex.at[:, pl.ds(p, 1)], exch_hbm.at[:, pl.ds(p, 1)], out_sem.at[slot]
        )

    for p in range(1, planes - 1):
        out_copy(p, p).start()
    fourth(2, m)

    for at, entry in enumerate(schedule):
        local = ewait(entry)
        if at + 1 < len(schedule):
            esend(schedule[at + 1], local)
    energy_ref[0] = (-0.5 / cells) * jnp.sum(local)

    arrived(4)
    for side in (LO, HI):
        p = 2 if side == LO else m
        step = -1 if side == LO else 1
        factor = c[p] * c[p + step] * c[p + 2 * step]
        total = sum((occ[b] * psi[b, p]) * urecv[side, b] for b in range(nb))
        total = total * factor
        for b in range(nb):
            ex[b, p - 2] = ex[b, p - 2] - total * urecv[side, b]
    for p in (0, planes - 1):
        out_copy(p, p).start()

    for number in range(5):
        for side in (LO, HI):
            @pl.when(has[1 - side])
            def _():
                copy(side, number).wait_send()
    if ngrp == 2:
        for depth in (1, 2):
            for side in (LO, HI):
                @pl.when(has[side])
                def _():
                    forward(side, depth, mine).wait_send()
    for number, base, radix, digit, peers in schedule:
        for k, other, peer in peers:
            ecopy(number, base, digit, k, digit, peer).wait_send()
    for p in range(planes):
        out_copy(p, p).wait()


def body(orbitals, band_ids, occupations, screen):
    nb, planes, gy, gz = orbitals.shape
    ngrp, n = lax.axis_size("grp"), lax.axis_size("band")
    npairs = nb * (nb + 1) // 2
    slots = sum(radices_of(n)) + 1
    f32 = jnp.float32
    dma = pltpu.SemaphoreType.DMA
    exchange, energy = pl.pallas_call(
        functools.partial(kernel, (ngrp, n, nb, planes, gy, gz), float(planes * n * gy * gz)),
        out_shape=(
            jax.ShapeDtypeStruct((nb, planes, gy, gz), f32),
            jax.ShapeDtypeStruct((1,), f32),
        ),
        in_specs=[
            pl.BlockSpec(memory_space=pl.ANY),
            pl.BlockSpec(memory_space=pl.ANY),
            pl.BlockSpec(memory_space=pltpu.SMEM),
            pl.BlockSpec(memory_space=pltpu.SMEM),
        ],
        out_specs=(pl.BlockSpec(memory_space=pl.ANY), pl.BlockSpec(memory_space=pltpu.SMEM)),
        scratch_shapes=[
            pltpu.VMEM((nb, planes + 4, gy, gz), f32),
            pltpu.VMEM((planes, gy, gz), f32),
            pltpu.VMEM((planes + 4, gy, gz), f32),
            pltpu.VMEM((2, nb, gy, gz), f32),
            pltpu.VMEM((2, nb, gy, gz), f32),
            pltpu.VMEM((npairs, planes + 4, gy + 2 * PAD, gz), f32),
            pltpu.VMEM((npairs, planes + 4, gy + 2 * PAD, gz), f32),
            pltpu.VMEM((npairs, planes + 2, gy + 2 * PAD, gz), f32),
            pltpu.VMEM((nb, planes, gy, gz), f32),
            pltpu.VMEM((slots, 8, gz), f32),
            dma((2,)),
            dma((planes,)),
            dma((2, 5)),
            dma((2, 5)),
            dma((2, 2)),
            dma((2, 2)),
            dma((slots,)),
            dma((slots,)),
        ],
        compiler_params=pltpu.CompilerParams(
            collective_id=0, has_side_effects=True, vmem_limit_bytes=63 * 1024 * 1024
        ),
    )(orbitals, screen, band_ids, occupations)
    return exchange, energy


def solution(mesh):
    in_specs = (P("grp", "band", None, None), P("grp"), P("grp"), P("band", None, None))
    out_specs = (P("grp", "band", None, None), P("grp"))
    return jax.shard_map(body, mesh=mesh, in_specs=in_specs, out_specs=out_specs, check_vma=False)
```

time: 109 us -> 42.2 us (0.39)
  blocking collectives: 45.6 us -> 0 us
  Pallas kernels: 0 us -> 37.6 us
  starting transfers between devices: 33.9 us -> 0 us
  other arithmetic: 22.2 us -> 0 us
  waiting for transfers between devices: 4.34 us -> 0 us
  local copies, waits for them, and re-layouts: 0.78 us -> 2.06 us
    psum x1 -> x0, blocking collectives: 45.6 us -> none  [body(): energy = lax.psum(local, 'band')]
    pallas_call x0 -> x1, Pallas kernels: none -> 37.6 us  [body(): pl.pallas_call(functools.partial(kernel, (ngrp, n, nb, planes, gy, gz), f...]
    ppermute x6 -> x0, starting transfers between devices: 33.9 us -> none  [the longest x3 30 us: padded_2(): lax.ppermute(lax.slice_in_dim(block, block.shape[dim] - width, None, axis...]
    concatenate x3 -> x0, other arithmetic: 9.42 us -> none  [padded_2(): block = jnp.concatenate([low, block, high], axis=dim)]
    add x3 -> x0, other arithmetic: 5.79 us -> none  [the longest x2 5.71 us: relax(): return phi + 0.8 * (rho - (diag * phi - near)) / diag]
    reduce_sum x3 -> x0, other arithmetic: 4.47 us -> none  [the longest x1 2.74 us: body(): exchange = -jnp.sum(weighted[None] * phi, axis=1)]
    ppermute x6 -> x0, waiting for transfers between devices: 4.34 us -> none  [the longest x3 4.33 us: padded_2(): lax.ppermute(lax.slice_in_dim(block, block.shape[dim] - width, None, axis...]
    unnamed x6 -> x1, local copies, waits for them, and re-layouts: 0.02 us -> 2.06 us
  transfers between devices with their start and end apart: 6 -> 0, of which waited for: 3 -> 0; matrix products, arithmetic and copies ran while one was open for 0% -> 0% of each run, Pallas kernels for 0% -> 0%
where the time goes in v1:
time: 42.2 us; the launch traced here: 42 us
  Pallas kernels  37.6 us (89%)
  between operations  2.32 us (5%)
  local copies, waits for them, and re-layouts  2.06 us (5%)
    pallas_call x1, Pallas kernels, body(): pl.pallas_call(functools.partial(kernel, (ngrp, n, nb, planes, gy, gz), f...  37.6 us
    unnamed x1, local copies, waits for them, and re-layouts  2.06 us

profile of v1, /device:TPU:0, one launch (start us, length us, event | category | flops | bytes accessed | tf_op | source)
XLA Modules:
  0.0 42.0 jit_solution(963771508250015567)
XLA Ops:
  0.6 37.6 %shard_map.59 = (f32[3,4,128,128]{3,2,1,0:T(8,128)}, f32[1]{0:T(128)}) custom-call(f32[3,4,128,128]{3,2,1,0:T(8,128)} %psi_hbm.1, f32[4,128,128]{2,1,0:T(8,128)} %screen_hbm.1, s32[3]{0:T(128)} %ids_ref.1, f32[3]{0:T(128)} %occs_ref.1), custom_call_target="tpu_custom_call" | custom-call | tf_op jit(solution)/shard_map/pallas_call | solution.py:374
  38.3 2.1 %copy.8 = f32[3,4,128,128]{3,2,1,0:T(8,128)} copy(f32[3,4,128,128]{3,2,1,0:T(8,128)} %get-tuple-element.4) | data formatting | bytes 1572864

commit v2 on v1

--- a/solution.py
+++ b/solution.py
@@ -9,15 +9,6 @@
 
 LO, HI = 0, 1
 PAD = 8
-
-
-def radices_of(count):
-    out = []
-    while count > 1:
-        radix = 4 if count % 4 == 0 else (2 if count % 2 == 0 else count)
-        out.append(radix)
-        count //= radix
-    return out
 
 
 def kernel(
@@ -32,39 +23,23 @@
     grp = lax.axis_index("grp")
     has = (me > 0, me < n - 1)
     near = (me - 1, me + 1)
-    radices = radices_of(n)
 
     load_psi = pltpu.make_async_copy(psi_hbm, psi.at[:, pl.ds(2, planes)], local_sem.at[0])
     load_scr = pltpu.make_async_copy(screen_hbm, scr, local_sem.at[1])
     load_scr.start()
     load_psi.start()
 
-    def rounds():
-        stride, base = 1, 0
-        for number, radix in enumerate(radices):
-            digit = (me // stride) % radix
-            peers = []
-            for k in range(1, radix):
-                other = (digit + k) % radix
-                peers.append((k, other, me + (other - digit) * stride))
-            yield number, base, radix, digit, peers
-            base += radix
-            stride *= radix
-
     barrier = pltpu.get_barrier_semaphore()
-    for side in (LO, HI):
-        @pl.when(has[side])
-        def _():
-            pl.semaphore_signal(barrier, inc=1, device_id={"band": near[side]})
     others = 0
     if ngrp == 2:
         pl.semaphore_signal(barrier, inc=1, device_id={"grp": 1 - grp})
         others += 1
-    for _, _, _, _, peers in rounds():
-        for _, _, peer in peers:
-            pl.semaphore_signal(barrier, inc=1, device_id={"band": peer})
-            others += 1
-    pl.semaphore_wait(barrier, others + has[LO].astype(jnp.int32) + has[HI].astype(jnp.int32))
+    def greet(k, carry):
+        pl.semaphore_signal(barrier, inc=1, device_id={"band": lax.rem(me + k, n)})
+        return carry
+
+    lax.fori_loop(1, n, greet, 0)
+    others += n - 1
 
     rows = gy // 2 if ngrp == 2 else gy
     mine = pl.ds(pl.multiple_of(grp * rows, 8), rows) if ngrp == 2 else pl.ds(0, gy)
@@ -124,22 +99,15 @@
                 def _():
                     forward(side, depth, theirs).wait_recv()
 
-    send(0)
     load_scr.wait()
-    for p in (0, planes - 1):
+    for p in range(planes):
         c[p + 2] = 0.8 / (6.0 + scr[p])
-    send(1)
-    send(2)
-    for p in range(1, planes - 1):
-        c[p + 2] = 0.8 / (6.0 + scr[p])
-    send(3)
     load_psi.wait()
     for side in (LO, HI):
         p = own(side, 3) + 2
         root = jnp.sqrt(c[p])
         for b in range(nb):
             usend[side, b] = root * psi[b, p]
-    send(4)
 
     for side in (LO, HI):
         @pl.when(jnp.logical_not(has[side]))
@@ -171,19 +139,12 @@
 
         lax.fori_loop(0, count, clear, 0)
 
+    pl.semaphore_wait(barrier, others)
+    for number in (1, 0, 3, 2, 4):
+        send(number)
+
     lanes = lax.broadcasted_iota(jnp.int32, (gy, gz), 1)
     first, last = lanes == 0, lanes == gz - 1
-
-    def pair_of(k):
-        i = jnp.int32(0)
-        start = jnp.int32(0)
-        at = 0
-        for b in range(1, nb):
-            at += nb - b + 1
-            over = (k >= at).astype(jnp.int32)
-            i = i + over
-            start = start + over * (nb - b + 1)
-        return i, i + k - start
 
     def lateral(buf, k, at):
         mid = buf[k, at, pl.ds(PAD, gy)]
@@ -203,12 +164,8 @@
         return each
 
     def pairwise(body):
-        def step(k, carry):
-            i, j = pair_of(k)
+        for k, (i, j) in enumerate(pairs):
             body(k, i, j)
-            return carry
-
-        lax.fori_loop(0, len(pairs), step, 0)
 
     def start_sweep(lo, hi):
         def plane(p, t):
@@ -276,44 +233,32 @@
     third(2, m)
 
     def energy_plane(p, acc):
-        def one(k, acc):
-            i, j = pair_of(k)
+        inverse = 1.25 * (6.0 + scr[p - 2])
+        for k, (i, j) in enumerate(pairs):
             a, b, d = (buf[k, at, pl.ds(PAD, gy)] for buf, at in ((f1, p), (f2, p), (f3, p - 1)))
-            weight = jnp.float32(0.0)
-            for number, (x, y) in enumerate(pairs):
-                weight = jnp.where(k == number, (1.0 if x == y else 2.0) * occ[x] * occ[y], weight)
-            value = psi[i, p] * psi[j, p] * b + (b - a) * (d - a) * (1.25 * (6.0 + scr[p - 2]))
-            return acc + weight * jnp.sum(value.reshape(gy // 8, 8, gz), axis=0)
-
-        return lax.fori_loop(0, len(pairs), one, acc)
+            weight = (1.0 if i == j else 2.0) * occ[i] * occ[j]
+            value = psi[i, p] * psi[j, p] * b + (b - a) * (d - a) * inverse
+            acc = acc + weight * jnp.sum(value.reshape(gy // 8, 8, gz), axis=0)
+        return acc
 
     local = lax.fori_loop(2, planes + 2, energy_plane, jnp.zeros((8, gz), jnp.float32))
 
-    def ecopy(number, base, digit, k, slot, peer):
+    def ecopy(slot, k):
         return pltpu.make_async_remote_copy(
-            src_ref=eslots.at[base + digit], dst_ref=eslots.at[base + slot],
-            send_sem=esend_sem.at[base + k], recv_sem=erecv_sem.at[base + slot],
-            device_id={"band": peer},
+            src_ref=eslots.at[me, pl.ds(0, 1)], dst_ref=eslots.at[slot, pl.ds(0, 1)],
+            send_sem=esend_sem.at[k], recv_sem=erecv_sem.at[slot],
+            device_id={"band": lax.rem(me + k, n)},
         )
 
-    def esend(entry, value):
-        number, base, radix, digit, peers = entry
-        eslots[base + digit] = value
-        for k, other, peer in peers:
-            ecopy(number, base, digit, k, digit, peer).start()
-
-    def ewait(entry):
-        number, base, radix, digit, peers = entry
-        for k, other, peer in peers:
-            ecopy(number, base, digit, k, other, peer).wait_recv()
-        total = eslots[base]
-        for r in range(1, radix):
-            total = total + eslots[base + r]
-        return total
-
-    schedule = list(rounds())
-    if schedule:
-        esend(schedule[0], local)
+    def each_peer(act):
+        def step(k, carry):
+            act(k)
+            return carry
+
+        lax.fori_loop(1, n, step, 0)
+
+    eslots[me, pl.ds(0, 1)] = jnp.sum(local, axis=0, keepdims=True)
+    each_peer(lambda k: ecopy(me, k).start())
 
     second(0, m + 2, outer=True)
     third(1, m + 1)
@@ -327,12 +272,6 @@
     for p in range(1, planes - 1):
         out_copy(p, p).start()
     fourth(2, m)
-
-    for at, entry in enumerate(schedule):
-        local = ewait(entry)
-        if at + 1 < len(schedule):
-            esend(schedule[at + 1], local)
-    energy_ref[0] = (-0.5 / cells) * jnp.sum(local)
 
     arrived(4)
     for side in (LO, HI):
@@ -357,9 +296,9 @@
                 @pl.when(has[side])
                 def _():
                     forward(side, depth, mine).wait_send()
-    for number, base, radix, digit, peers in schedule:
-        for k, other, peer in peers:
-            ecopy(number, base, digit, k, digit, peer).wait_send()
+    each_peer(lambda k: ecopy(lax.rem(me + k, n), k).wait_recv())
+    energy_ref[0] = (-0.5 / cells) * jnp.sum(eslots[:, pl.ds(0, 1)])
+    each_peer(lambda k: ecopy(me, k).wait_send())
     for p in range(planes):
         out_copy(p, p).wait()
 
@@ -368,7 +307,7 @@
     nb, planes, gy, gz = orbitals.shape
     ngrp, n = lax.axis_size("grp"), lax.axis_size("band")
     npairs = nb * (nb + 1) // 2
-    slots = sum(radices_of(n)) + 1
+    slots = n
     f32 = jnp.float32
     dma = pltpu.SemaphoreType.DMA
     exchange, energy = pl.pallas_call(

time: 42.2 us -> 36.6 us (0.87)
  Pallas kernels: 37.6 us -> 32 us
    pallas_call x1, Pallas kernels: 37.6 us -> 32 us  [body(): pl.pallas_call(functools.partial(kernel, (ngrp, n, nb, planes, gy, gz), f...]
where the time goes in v2:
time: 36.6 us; the launch traced here: 36.3 us
  Pallas kernels  32 us (87%)
  between operations  2.32 us (6%)
  local copies, waits for them, and re-layouts  2.06 us (6%)
    pallas_call x1, Pallas kernels, body(): pl.pallas_call(functools.partial(kernel, (ngrp, n, nb, planes, gy, gz), f...  32 us
    unnamed x1, local copies, waits for them, and re-layouts  2.06 us

profile of v2, /device:TPU:0, one launch (start us, length us, event | category | flops | bytes accessed | tf_op | source)
XLA Modules:
  0.0 36.3 jit_solution(16755227738641915139)
XLA Ops:
  0.6 32.0 %shard_map.59 = (f32[3,4,128,128]{3,2,1,0:T(8,128)}, f32[1]{0:T(128)}) custom-call(f32[3,4,128,128]{3,2,1,0:T(8,128)} %psi_hbm.1, f32[4,128,128]{2,1,0:T(8,128)} %screen_hbm.1, s32[3]{0:T(128)} %ids_ref.1, f32[3]{0:T(128)} %occs_ref.1), custom_call_target="tpu_custom_call" | custom-call | tf_op jit(solution)/shard_map/pallas_call | solution.py:313
  32.6 2.1 %copy.8 = f32[3,4,128,128]{3,2,1,0:T(8,128)} copy(f32[3,4,128,128]{3,2,1,0:T(8,128)} %get-tuple-element.4) | data formatting | bytes 1572864

commit v3 on v2

--- a/solution.py
+++ b/solution.py
@@ -31,7 +31,7 @@
 
     barrier = pltpu.get_barrier_semaphore()
     others = 0
-    if ngrp == 2:
+    if ngrp < 0:
         pl.semaphore_signal(barrier, inc=1, device_id={"grp": 1 - grp})
         others += 1
     def greet(k, carry):
@@ -41,9 +41,9 @@
     lax.fori_loop(1, n, greet, 0)
     others += n - 1
 
-    rows = gy // 2 if ngrp == 2 else gy
-    mine = pl.ds(pl.multiple_of(grp * rows, 8), rows) if ngrp == 2 else pl.ds(0, gy)
-    theirs = pl.ds(pl.multiple_of((1 - grp) * rows, 8), rows) if ngrp == 2 else pl.ds(0, gy)
+    rows = gy // 2 if ngrp < 0 else gy
+    mine = pl.ds(pl.multiple_of(grp * rows, 8), rows) if ngrp < 0 else pl.ds(0, gy)
+    theirs = pl.ds(pl.multiple_of((1 - grp) * rows, 8), rows) if ngrp < 0 else pl.ds(0, gy)
 
     def halo(side, depth):
         return 2 - depth if side == LO else planes + 1 + depth
@@ -73,6 +73,12 @@
             def _():
                 copy(side, number).start()
 
+    def sent(number):
+        for side in (LO, HI):
+            @pl.when(has[1 - side])
+            def _():
+                copy(side, number).wait_send()
+
     def arrived(number):
         for side in (LO, HI):
             @pl.when(has[side])
@@ -89,7 +95,7 @@
 
     def screen_arrived(depth):
         arrived(2 * depth - 1)
-        if ngrp == 2:
+        if ngrp < 0:
             for side in (LO, HI):
                 @pl.when(has[side])
                 def _():
@@ -140,7 +146,7 @@
         lax.fori_loop(0, count, clear, 0)
 
     pl.semaphore_wait(barrier, others)
-    for number in (1, 0, 3, 2, 4):
+    for number in (1, 0, 3, 2):
         send(number)
 
     lanes = lax.broadcasted_iota(jnp.int32, (gy, gz), 1)
@@ -226,6 +232,8 @@
     start_sweep(1, m + 1)
     second(2, m)
     third(3, m - 1)
+    sent(2)
+    send(4)
     arrived(2)
     screen_arrived(2)
     start_sweep(0, m + 2)
@@ -285,12 +293,9 @@
     for p in (0, planes - 1):
         out_copy(p, p).start()
 
-    for number in range(5):
-        for side in (LO, HI):
-            @pl.when(has[1 - side])
-            def _():
-                copy(side, number).wait_send()
-    if ngrp == 2:
+    for number in (0, 1, 3, 4):
+        sent(number)
+    if ngrp < 0:
         for depth in (1, 2):
             for side in (LO, HI):
                 @pl.when(has[side])

time: 36.6 us -> 32.7 us (0.89)
  Pallas kernels: 32 us -> 28.1 us
    pallas_call x1, Pallas kernels: 32 us -> 28.1 us  [body(): pl.pallas_call(functools.partial(kernel, (ngrp, n, nb, planes, gy, gz), f...]
where the time goes in v3:
time: 32.7 us; the launch traced here: 32.5 us
  Pallas kernels  28.1 us (86%)
  between operations  2.32 us (7%)
  local copies, waits for them, and re-layouts  2.06 us (6%)
    pallas_call x1, Pallas kernels, body(): pl.pallas_call(functools.partial(kernel, (ngrp, n, nb, planes, gy, gz), f...  28.1 us
    unnamed x1, local copies, waits for them, and re-layouts  2.06 us

profile of v3, /device:TPU:0, one launch (start us, length us, event | category | flops | bytes accessed | tf_op | source)
XLA Modules:
  0.0 32.5 jit_solution(9488020554683579924)
XLA Ops:
  0.6 28.1 %shard_map.59 = (f32[3,4,128,128]{3,2,1,0:T(8,128)}, f32[1]{0:T(128)}) custom-call(f32[3,4,128,128]{3,2,1,0:T(8,128)} %psi_hbm.1, f32[4,128,128]{2,1,0:T(8,128)} %screen_hbm.1, s32[3]{0:T(128)} %ids_ref.1, f32[3]{0:T(128)} %occs_ref.1), custom_call_target="tpu_custom_call" | custom-call | tf_op jit(solution)/shard_map/pallas_call | solution.py:318
  28.7 2.1 %copy.8 = f32[3,4,128,128]{3,2,1,0:T(8,128)} copy(f32[3,4,128,128]{3,2,1,0:T(8,128)} %get-tuple-element.4) | data formatting | bytes 1572864

commit v4 on v3

--- a/solution.py
+++ b/solution.py
@@ -31,7 +31,7 @@
 
     barrier = pltpu.get_barrier_semaphore()
     others = 0
-    if ngrp < 0:
+    if ngrp == 2:
         pl.semaphore_signal(barrier, inc=1, device_id={"grp": 1 - grp})
         others += 1
     def greet(k, carry):
@@ -41,9 +41,9 @@
     lax.fori_loop(1, n, greet, 0)
     others += n - 1
 
-    rows = gy // 2 if ngrp < 0 else gy
-    mine = pl.ds(pl.multiple_of(grp * rows, 8), rows) if ngrp < 0 else pl.ds(0, gy)
-    theirs = pl.ds(pl.multiple_of((1 - grp) * rows, 8), rows) if ngrp < 0 else pl.ds(0, gy)
+    rows = gy // 2 if ngrp == 2 else gy
+    mine = pl.ds(pl.multiple_of(grp * rows, 8), rows) if ngrp == 2 else pl.ds(0, gy)
+    theirs = pl.ds(pl.multiple_of((1 - grp) * rows, 8), rows) if ngrp == 2 else pl.ds(0, gy)
 
     def halo(side, depth):
         return 2 - depth if side == LO else planes + 1 + depth
@@ -59,8 +59,9 @@
             src = psi_hbm.at[:, pl.ds(own(side, depth), 1)]
             dst = psi.at[:, pl.ds(halo(side, depth), 1)]
         else:
-            src = c.at[own(side, depth) + 2, mine]
-            dst = c.at[halo(side, depth), mine]
+            part = mine
+            src = c.at[own(side, depth) + 2, part]
+            dst = c.at[halo(side, depth), part]
         return pltpu.make_async_remote_copy(
             src_ref=src, dst_ref=dst,
             send_sem=send_sem.at[side, number], recv_sem=recv_sem.at[side, number],
@@ -93,17 +94,12 @@
             device_id={"grp": 1 - grp},
         )
 
-    def screen_arrived(depth):
-        arrived(2 * depth - 1)
-        if ngrp < 0:
+    def halves(act):
+        if ngrp == 2:
             for side in (LO, HI):
                 @pl.when(has[side])
                 def _():
-                    forward(side, depth, mine).start()
-            for side in (LO, HI):
-                @pl.when(has[side])
-                def _():
-                    forward(side, depth, theirs).wait_recv()
+                    act(side)
 
     load_scr.wait()
     for p in range(planes):
@@ -146,7 +142,7 @@
         lax.fori_loop(0, count, clear, 0)
 
     pl.semaphore_wait(barrier, others)
-    for number in (1, 0, 3, 2):
+    for number in (1, 3, 0):
         send(number)
 
     lanes = lax.broadcasted_iota(jnp.int32, (gy, gz), 1)
@@ -227,15 +223,19 @@
     start_sweep(2, m)
     start_sweep(3, m - 1)
     second(3, m - 1)
+    for depth in (1, 2):
+        arrived(2 * depth - 1)
+        halves(lambda side: forward(side, depth, mine).start())
+    send(2)
     arrived(0)
-    screen_arrived(1)
+    halves(lambda side: forward(side, 1, theirs).wait_recv())
     start_sweep(1, m + 1)
     second(2, m)
     third(3, m - 1)
     sent(2)
     send(4)
     arrived(2)
-    screen_arrived(2)
+    halves(lambda side: forward(side, 2, theirs).wait_recv())
     start_sweep(0, m + 2)
     second(1, m + 1)
     third(2, m)
@@ -295,12 +295,8 @@
 
     for number in (0, 1, 3, 4):
         sent(number)
-    if ngrp < 0:
-        for depth in (1, 2):
-            for side in (LO, HI):
-                @pl.when(has[side])
-                def _():
-                    forward(side, depth, mine).wait_send()
+    for depth in (1, 2):
+        halves(lambda side: forward(side, depth, mine).wait_send())
     each_peer(lambda k: ecopy(lax.rem(me + k, n), k).wait_recv())
     energy_ref[0] = (-0.5 / cells) * jnp.sum(eslots[:, pl.ds(0, 1)])
     each_peer(lambda k: ecopy(me, k).wait_send())

time: 32.7 us -> 31.3 us (0.957)
  Pallas kernels: 28.1 us -> 26.7 us
    pallas_call x1, Pallas kernels: 28.1 us -> 26.7 us  [body(): pl.pallas_call(functools.partial(kernel, (ngrp, n, nb, planes, gy, gz), f...]
where the time goes in v4:
time: 31.3 us; the launch traced here: 31.1 us
  Pallas kernels  26.7 us (85%)
  between operations  2.32 us (7%)
  local copies, waits for them, and re-layouts  2.06 us (7%)
    pallas_call x1, Pallas kernels, body(): pl.pallas_call(functools.partial(kernel, (ngrp, n, nb, planes, gy, gz), f...  26.7 us
    unnamed x1, local copies, waits for them, and re-layouts  2.06 us

profile of v4, /device:TPU:0, one launch (start us, length us, event | category | flops | bytes accessed | tf_op | source)
XLA Modules:
  0.0 31.1 jit_solution(10154299441134391554)
XLA Ops:
  0.6 26.7 %shard_map.59 = (f32[3,4,128,128]{3,2,1,0:T(8,128)}, f32[1]{0:T(128)}) custom-call(f32[3,4,128,128]{3,2,1,0:T(8,128)} %psi_hbm.1, f32[4,128,128]{2,1,0:T(8,128)} %screen_hbm.1, s32[3]{0:T(128)} %ids_ref.1, f32[3]{0:T(128)} %occs_ref.1), custom_call_target="tpu_custom_call" | custom-call | tf_op jit(solution)/shard_map/pallas_call | solution.py:314
  27.3 2.1 %copy.8 = f32[3,4,128,128]{3,2,1,0:T(8,128)} copy(f32[3,4,128,128]{3,2,1,0:T(8,128)} %get-tuple-element.4) | data formatting | bytes 1572864

commit v5 on v4

--- a/solution.py
+++ b/solution.py
@@ -53,8 +53,9 @@
 
     def copy(side, number):
         depth = number // 2 + 1
-        if number == 4:
-            src, dst = usend.at[side], urecv.at[side]
+        if number >= 4:
+            some = pl.ds(0, nb - 1) if number == 4 else pl.ds(nb - 1, 1)
+            src, dst = usend.at[side, some], urecv.at[side, some]
         elif number % 2 == 0:
             src = psi_hbm.at[:, pl.ds(own(side, depth), 1)]
             dst = psi.at[:, pl.ds(halo(side, depth), 1)]
@@ -227,6 +228,7 @@
         arrived(2 * depth - 1)
         halves(lambda side: forward(side, depth, mine).start())
     send(2)
+    send(5)
     arrived(0)
     halves(lambda side: forward(side, 1, theirs).wait_recv())
     start_sweep(1, m + 1)
@@ -282,6 +284,7 @@
     fourth(2, m)
 
     arrived(4)
+    arrived(5)
     for side in (LO, HI):
         p = 2 if side == LO else m
         step = -1 if side == LO else 1
@@ -293,7 +296,7 @@
     for p in (0, planes - 1):
         out_copy(p, p).start()
 
-    for number in (0, 1, 3, 4):
+    for number in (0, 1, 3, 4, 5):
         sent(number)
     for depth in (1, 2):
         halves(lambda side: forward(side, depth, mine).wait_send())
@@ -337,8 +340,8 @@
             pltpu.VMEM((slots, 8, gz), f32),
             dma((2,)),
             dma((planes,)),
-            dma((2, 5)),
-            dma((2, 5)),
+            dma((2, 6)),
+            dma((2, 6)),
             dma((2, 2)),
             dma((2, 2)),
             dma((slots,)),

time: 31.3 us -> 31.3 us (level)
  no operation moved by 1% of the time
where the time goes in v5:
time: 31.3 us; the launch traced here: 31.1 us
  Pallas kernels  26.7 us (85%)
  between operations  2.32 us (7%)
  local copies, waits for them, and re-layouts  2.06 us (7%)
    pallas_call x1, Pallas kernels, body(): pl.pallas_call(functools.partial(kernel, (ngrp, n, nb, planes, gy, gz), f...  26.7 us
    unnamed x1, local copies, waits for them, and re-layouts  2.06 us

profile of v5, /device:TPU:0, one launch (start us, length us, event | category | flops | bytes accessed | tf_op | source)
XLA Modules:
  0.0 31.1 jit_solution(16535467045805464777)
XLA Ops:
  0.6 26.7 %shard_map.59 = (f32[3,4,128,128]{3,2,1,0:T(8,128)}, f32[1]{0:T(128)}) custom-call(f32[3,4,128,128]{3,2,1,0:T(8,128)} %psi_hbm.1, f32[4,128,128]{2,1,0:T(8,128)} %screen_hbm.1, s32[3]{0:T(128)} %ids_ref.1, f32[3]{0:T(128)} %occs_ref.1), custom_call_target="tpu_custom_call" | custom-call | tf_op jit(solution)/shard_map/pallas_call | solution.py:317
  27.4 2.1 %copy.8 = f32[3,4,128,128]{3,2,1,0:T(8,128)} copy(f32[3,4,128,128]{3,2,1,0:T(8,128)} %get-tuple-element.4) | data formatting | bytes 1572864
